TPU v7x, 32 devices: a whole 2x2x4 slice. The times are simulated.
32 devices in a mesh: domain: 8 (over z, x), band: 4 (over y, core).
Axes of the slice: x: 2, y: 2, z: 4, core: 2. Of those that a mesh axis runs over, the one named last changes fastest.
Arguments:
- wavefunctions: bfloat16 [32000, 1024], P('domain', 'band'), may hold values from -6 to 6
- potential: float32 [32000], P('domain'), may hold values from -1.5 to 0.5
- cell_matrix: bfloat16 [125, 125], replicated, may hold values from -0.5 to 0.5
- neighbours: int32 [256, 6], P('domain'), may hold values from 0 to 63, as said below
- window: float32 [2], replicated, may hold values from -1.6 to 5.6, as said below
Outputs:
- filtered: bfloat16 [32000, 1024], P('domain', 'band')
- projected: float32 [1024, 1024], P('band')
Inputs may be any that keep to these rules, and one draw needn't show every extreme that they name: `neighbours`: the cells form a periodic grid of 4 x 4 x (16) cells, domain g holding z layers g * 2 to g * 2 + 1; slots 0 to 15 of a domain are its lowest layer and the last 16 slots its highest, in a drawn order, the rest in a drawn order. Faces pair up: if cell a meets cell b across face d, b meets a across d xor 1. window[0] < window[1], and every eigenvalue of H lies below window[1].
All inputs are finite; a program needn't handle non-finite values.
Results may differ from a plain program's by a relative error of at most 0.01.
The roundings to bfloat16 on the way count: a program that leaves them out, or rounds other values in their place, can miss the bound.
Values may be sent and summed in bfloat16 or wider, within the bound.
A program may use at most 128 MiB of HBM per device.

v0:
```python
import jax
import jax.numpy as jnp
import numpy as np
from jax import lax
from jax.sharding import PartitionSpec as P

NPC = 125
SIDE = 4


penalty = 0.5
highest = lax.Precision.HIGHEST


def padded(cells, sides, width):
    for axis, dim in sides:
        count = lax.axis_size(axis)
        head = lax.slice_in_dim(cells, 0, width, axis=dim)
        tail = lax.slice_in_dim(cells, cells.shape[dim] - width, cells.shape[dim], axis=dim)
        cells = jnp.concatenate(
            [
                lax.ppermute(tail, axis, [(i, (i + 1) % count) for i in range(count)]),
                cells,
                lax.ppermute(head, axis, [((i + 1) % count, i) for i in range(count)]),
            ],
            axis=dim,
        )
    return cells


def face_table():
    incidence = np.zeros((125, 150), np.float32)
    for direction in range(6):
        axis_index = direction // 2
        level = 4 * (direction % 2)
        for first in range(5):
            for second in range(5):
                others = [first, second]
                coords = others[:axis_index] + [level] + others[axis_index:]
                node = 25 * coords[0] + 5 * coords[1] + coords[2]
                incidence[node, 25 * direction + 5 * first + second] = 1.0
    return incidence


def face_view(field, direction):
    return lax.index_in_dim(field, 4 * (direction % 2), 1 + direction // 2, keepdims=False)


def apply_operator(values, combined, node_weight, neighbours):
    cell_count = neighbours.shape[0]
    columns = values.shape[1]
    face_cells = SIDE * SIDE
    shaped = values.reshape(cell_count, 5, 5, 5, columns)
    rim_pair = jnp.concatenate(
        [shaped[:face_cells, :, :, 0], shaped[cell_count - face_cells :, :, :, 4]], axis=0
    )
    rims = padded(rim_pair, (("domain", 0),), face_cells)
    from_below = rims[:face_cells]
    from_above = rims[3 * face_cells :]
    pieces = [values.reshape(cell_count, NPC, columns)]
    for direction in range(6):
        table = jnp.concatenate([face_view(shaped, direction ^ 1), from_below, from_above], axis=0)
        nearby = jnp.take(table, neighbours[:, direction], axis=0)
        pieces.append(nearby.reshape(cell_count, 25, columns))
    stacked = jnp.concatenate(pieces, axis=1)
    result = jnp.einsum("mn,cnb->cmb", combined, stacked, preferred_element_type=jnp.float32)
    result = result + node_weight[:, :, None] * pieces[0].astype(jnp.float32)
    return result.reshape(cell_count * NPC, columns)


def per_device(wavefunctions, potential, cell_matrix, neighbours, window):
    wide = cell_matrix.astype(jnp.float32)
    stiffness = ((wide + wide.T) * 0.5).astype(jnp.bfloat16)
    incidence = jnp.asarray(face_table())
    combined = jnp.concatenate([stiffness, (-penalty * incidence).astype(jnp.bfloat16)], axis=1)
    cell_count = neighbours.shape[0]
    node_weight = potential.reshape(cell_count, NPC) + penalty * jnp.sum(incidence, axis=1)[None, :]

    def operate(values):
        return apply_operator(values, combined, node_weight, neighbours)

    center = (window[0] + window[1]) * 0.5
    half = (window[1] - window[0]) * 0.5
    image = operate(wavefunctions)
    previous = wavefunctions
    current = ((image - center * wavefunctions.astype(jnp.float32)) / half).astype(jnp.bfloat16)
    for degree in range(3):
        image = operate(current)
        following = (
            2.0 * (image - center * current.astype(jnp.float32)) / half
            - previous.astype(jnp.float32)
        ).astype(jnp.bfloat16)
        previous, current = (current, following)
    image_last = operate(current).astype(jnp.bfloat16)
    row_block, image_rows = (
        lax.all_to_all(current, "band", split_axis=0, concat_axis=1, tiled=True),
        lax.all_to_all(image_last, "band", split_axis=0, concat_axis=1, tiled=True),
    )
    contract = (((0,), (0,)), ((), ()))
    margin_part = lax.dot_general(
        row_block, row_block, contract, preferred_element_type=jnp.float32
    )
    cross_part = lax.dot_general(
        row_block, image_rows, contract, preferred_element_type=jnp.float32
    )
    margin_sum, cross_sum = lax.psum((margin_part, cross_part), ("domain", "band"))
    total_rows = row_block.shape[0] * lax.axis_size("domain") * lax.axis_size("band")
    margin = margin_sum / total_rows
    cross = cross_sum / total_rows
    lower = jnp.linalg.cholesky(margin)
    inverse = jax.scipy.linalg.solve_triangular(
        lower, jnp.eye(margin.shape[0], dtype=jnp.float32), lower=True
    )
    rotated = lax.dot_general(
        row_block,
        inverse.astype(jnp.bfloat16),
        (((1,), (1,)), ((), ())),
        preferred_element_type=jnp.float32,
    ).astype(jnp.bfloat16)
    filtered = lax.all_to_all(rotated, "band", split_axis=1, concat_axis=0, tiled=True)
    row_count = filtered.shape[1]
    inverse_rows = lax.dynamic_slice_in_dim(
        inverse, lax.axis_index("band") * row_count, row_count, 0
    )
    left = jnp.dot(inverse_rows, cross, precision=highest, preferred_element_type=jnp.float32)
    projected = lax.dot_general(
        left,
        inverse,
        (((1,), (1,)), ((), ())),
        precision=highest,
        preferred_element_type=jnp.float32,
    )
    return (filtered, projected)


def solution(mesh):
    placed = (P("domain", "band"), P("domain"), P(), P("domain", None), P())
    return jax.shard_map(
        per_device,
        mesh=mesh,
        in_specs=placed,
        out_specs=(P("domain", "band"), P("band", None)),
        check_vma=False,
    )
```

profile of v0, /device:TPU:0, one launch (start us, length us, event | category | flops | bytes accessed | tf_op | source)
XLA Modules:
  0.0 1156.8 jit_solution(14712372045100997797)
XLA Ops:
  56.5 33.7 %concatenate.141 = bf16[32,275,256]{2,1,0:T(8,128)(2,1)} concatenate(bf16[32,125,256]{2,1,0:T(8,128)(2,1)S(1)} %copy-done.6, bf16[32,25,256]{2,1,0:T(8,128)(2,1)} %copy.227, bf16[32,25,256]{2,1,0:T(8,128)(2,1)S(1)} %copy-done.24, bf16[32,25,256]{2,1,0:T(8,128)(2,1)S(1)} %copy-done.29, bf16[32,25,256]{2,1,0:T(8,128)(2,1)} %copy.230, bf16[32,25,256]{2,1,0:T(8,128)(2,1)} %copy.231, ...), dimensions={1} | concatenate | bytes 9011200 | tf_op jit(solution)/shard_map/concatenate | solution.py:65
  90.2 5.9 bitcast_add_fusion.5
  106.4 5.4 fusion.108
  124.9 7.8 collective-permute-done.2
  168.1 37.7 %concatenate.149 = bf16[32,275,256]{2,1,0:T(8,128)(2,1)} concatenate(bf16[32,125,256]{2,1,0:T(8,128)(2,1)} %reshape.268, bf16[32,25,256]{2,1,0:T(8,128)(2,1)} %copy.246, bf16[32,25,256]{2,1,0:T(8,128)(2,1)S(1)} %copy-done.26, bf16[32,25,256]{2,1,0:T(8,128)(2,1)S(1)} %copy-done.30, bf16[32,25,256]{2,1,0:T(8,128)(2,1)} %copy.249, bf16[32,25,256]{2,1,0:T(8,128)(2,1)} %copy.250, ...), dimensions={1} | concatenate | bytes 9011200 | tf_op jit(solution)/shard_map/concatenate | solution.py:65
  205.8 6.5 bitcast_add_fusion.4
  216.2 5.1 fusion.7
  221.2 4.9 reshape.278
  226.1 5.4 fusion.106
  245.9 7.1 collective-permute-done.4
  289.0 37.7 %concatenate.156 = bf16[32,275,256]{2,1,0:T(8,128)(2,1)} concatenate(bf16[32,125,256]{2,1,0:T(8,128)(2,1)} %reshape.277, bf16[32,25,256]{2,1,0:T(8,128)(2,1)} %copy.264, bf16[32,25,256]{2,1,0:T(8,128)(2,1)S(1)} %copy-done.27, bf16[32,25,256]{2,1,0:T(8,128)(2,1)S(1)} %copy-done.31, bf16[32,25,256]{2,1,0:T(8,128)(2,1)} %copy.267, bf16[32,25,256]{2,1,0:T(8,128)(2,1)} %copy.268, ...), dimensions={1} | concatenate | bytes 9011200 | tf_op jit(solution)/shard_map/concatenate | solution.py:65
  326.7 6.5 bitcast_add_fusion.3
  337.1 5.1 fusion.11
  342.2 4.9 reshape.287
  347.1 5.4 fusion.104
  368.8 7.1 collective-permute-done.6
  401.9 33.7 %concatenate.163 = bf16[32,275,256]{2,1,0:T(8,128)(2,1)} concatenate(bf16[32,125,256]{2,1,0:T(8,128)(2,1)S(1)} %copy-done.7, bf16[32,25,256]{2,1,0:T(8,128)(2,1)} %copy.282, bf16[32,25,256]{2,1,0:T(8,128)(2,1)S(1)} %copy-done.28, bf16[32,25,256]{2,1,0:T(8,128)(2,1)S(1)} %copy-done.32, bf16[32,25,256]{2,1,0:T(8,128)(2,1)} %copy.285, bf16[32,25,256]{2,1,0:T(8,128)(2,1)} %copy.286, ...), dimensions={1} | concatenate | bytes 9011200 | tf_op jit(solution)/shard_map/concatenate | solution.py:65
  435.6 5.9 bitcast_add_fusion.2
  445.4 5.1 fusion.15
  473.6 4.8 all-to-all-start
  509.6 33.7 %concatenate.170 = bf16[32,275,256]{2,1,0:T(8,128)(2,1)} concatenate(bf16[32,125,256]{2,1,0:T(8,128)(2,1)S(1)} %copy-done.10, bf16[32,25,256]{2,1,0:T(8,128)(2,1)} %copy.304, bf16[32,25,256]{2,1,0:T(8,128)(2,1)S(1)} %copy-done.23, bf16[32,25,256]{2,1,0:T(8,128)(2,1)S(1)} %copy-done.25, bf16[32,25,256]{2,1,0:T(8,128)(2,1)} %copy.307, bf16[32,25,256]{2,1,0:T(8,128)(2,1)} %copy.308, ...), dimensions={1} | concatenate | bytes 9011200 | tf_op jit(solution)/shard_map/concatenate | solution.py:65
  543.3 5.5 fusion
  559.2 6.5 fusion.113
  565.7 14.6 %all-to-all-done.2 = bf16[4,1000,256]{2,1,0:T(8,128)(2,1)S(1)} async-done(((bf16[4,1000,256]{2,1,0:T(8,128)(2,1)}), bf16[4,1000,256]{2,1,0:T(8,128)(2,1)S(1)}, u32[]{:S(2)}, u32[]{:S(2)}) %all-to-all-start.2) | async-done | bytes 2048032 | tf_op jit(solution)/shard_map/all_to_all | solution.py:97
  582.8 6.6 fusion.114
  592.9 172.1 %all-reduce.4.cloned.1.call-done = (f32[1024,1024]{0,1:T(8,128)}, f32[1024,1024]{0,1:T(8,128)}) async-done(((f32[1024,1024]{0,1:T(8,128)}, f32[1024,1024]{0,1:T(8,128)}), (f32[1024,1024]{0,1:T(8,128)}, f32[1024,1024]{0,1:T(8,128)})) %all-reduce.4.cloned.1.call-update) | async-done | bytes 8388624 | tf_op jit(solution)/shard_map/psum | solution.py:106
  765.0 5.1 broadcast_multiply_fusion
  770.1 5.5 copy.290
  782.1 11.7 %cholesky.223 = f32[128,128]{1,0:T(8,128)S(1)} custom-call(f32[128,128]{1,0:T(8,128)S(1)} %cholesky.580), custom_call_target="Cholesky" | custom-call | tf_op jit(solution)/shard_map/jit(cholesky)/cholesky | solution.py:110
  796.3 9.8 custom-call.63
  810.0 11.9 %cholesky.244 = f32[128,128]{1,0:T(8,128)S(1)} custom-call(f32[128,128]{1,0:T(8,128)S(1)} %cholesky.584), custom_call_target="Cholesky" | custom-call | tf_op jit(solution)/shard_map/jit(cholesky)/cholesky | solution.py:110
  823.9 9.8 custom-call.64
  837.1 11.7 %cholesky.468 = f32[128,128]{1,0:T(8,128)S(1)} custom-call(f32[128,128]{1,0:T(8,128)S(1)} %cholesky.589), custom_call_target="Cholesky" | custom-call | tf_op jit(solution)/shard_map/jit(cholesky)/cholesky | solution.py:110
  850.2 9.8 custom-call.65
  863.5 12.1 %cholesky.487 = f32[128,128]{1,0:T(8,128)S(1)} custom-call(f32[128,128]{1,0:T(8,128)S(1)} %cholesky.594), custom_call_target="Cholesky" | custom-call | tf_op jit(solution)/shard_map/jit(cholesky)/cholesky | solution.py:110
  876.9 9.8 custom-call.66
  890.2 11.7 %cholesky.506 = f32[128,128]{1,0:T(8,128)S(1)} custom-call(f32[128,128]{1,0:T(8,128)S(1)} %cholesky.599), custom_call_target="Cholesky" | custom-call | tf_op jit(solution)/shard_map/jit(cholesky)/cholesky | solution.py:110
  903.2 9.9 custom-call.67
  916.4 11.7 %cholesky.526 = f32[128,128]{1,0:T(8,128)S(1)} custom-call(f32[128,128]{1,0:T(8,128)S(1)} %cholesky.604), custom_call_target="Cholesky" | custom-call | tf_op jit(solution)/shard_map/jit(cholesky)/cholesky | solution.py:110
  929.5 9.8 custom-call.68
  942.5 11.9 %cholesky.546 = f32[128,128]{1,0:T(8,128)S(1)} custom-call(f32[128,128]{1,0:T(8,128)S(1)} %cholesky.609), custom_call_target="Cholesky" | custom-call | tf_op jit(solution)/shard_map/jit(cholesky)/cholesky | solution.py:110
  955.8 9.8 custom-call.69
  968.2 11.7 %cholesky.564 = f32[128,128]{1,0:T(8,128)S(1)} custom-call(f32[128,128]{1,0:T(8,128)S(1)} %convolution_subtract_fusion.11), custom_call_target="Cholesky" | custom-call | tf_op jit(solution)/shard_map/jit(cholesky)/cholesky | solution.py:110
  986.4 4.9 select_select_fusion
  991.3 23.2 %while.1 = (s32[]{:T(128)}, f32[1024,1024]{1,0:T(8,128)}, s32[8,2]{0,1:T(2,128)S(1)}, f32[8,128,128]{2,1,0:T(8,128)S(1)}, s32[]{:T(128)}) while((s32[]{:T(128)}, f32[1024,1024]{1,0:T(8,128)}, s32[8,2]{0,1:T(2,128)S(1)}, f32[8,128,128]{2,1,0:T(8,128)S(1)}, s32[]{:T(128)}) %tuple.127), condition=%wide.while_cond, body=%wide.while_body.sunk | while | flops 2 | bytes 131181 | solution.py:111
  1014.5 79.0 %custom-call.70 = f32[8,128,128]{1,2,0:T(8,128)S(1)} custom-call(f32[8,128,128]{2,1,0:T(8,128)S(1)} %get-tuple-element.10), custom_call_target="InvertDiagBlocksLowerTriangular" | custom-call | tf_op jit(solution)/shard_map/jit(_solve_triangular)/triangular_solve | solution.py:111
  1123.4 6.2 fusion.2
  1134.3 14.2 %all-to-all-done.1 = bf16[1000,4,256]{2,0,1:T(8,128)(2,1)S(1)} async-done(((bf16[1000,4,256]{2,0,1:T(8,128)(2,1)}), bf16[1000,4,256]{2,0,1:T(8,128)(2,1)S(1)}, u32[]{:S(2)}, u32[]{:S(2)}) %all-to-all-start.1) | async-done | bytes 2048032 | tf_op jit(solution)/shard_map/all_to_all | solution.py:120
  (377 shorter events, 380.5 us)
Async XLA Ops:
  10.7 8.6 copy-start.5
  12.5 21.4 %collective-permute-start = (bf16[16,5,5,256]{3,2,1,0:T(8,128)(2,1)}, bf16[16,5,5,256]{3,2,1,0:T(8,128)(2,1)}, u32[]{:S(2)}, u32[]{:S(2)}) collective-permute-start(bf16[16,5,5,256]{3,2,1,0:T(8,128)(2,1)} %bitcast.301), channel_id=1, source_target_pairs={{0,4},{4,8},{8,12},{12,16},{16,20},{20,24},{24,28},{28,0},{1,5},{5... | collective-permute-start | bytes 614408 | tf_op jit(solution)/shard_map/ppermute | solution.py:22
  16.2 17.7 %collective-permute-start.1 = (bf16[16,5,5,256]{3,2,1,0:T(8,128)(2,1)}, bf16[16,5,5,256]{3,2,1,0:T(8,128)(2,1)}, u32[]{:S(2)}, u32[]{:S(2)}) collective-permute-start(bf16[16,5,5,256]{3,2,1,0:T(8,128)(2,1)} %bitcast.300), channel_id=1, source_target_pairs={{4,0},{8,4},{12,8},{16,12},{20,16},{24,20},{28,24},{0,28},{5,1},{9... | collective-permute-start | bytes 614408 | tf_op jit(solution)/shard_map/ppermute | solution.py:24
  21.6 5.2 copy-start.1
  24.2 4.5 copy-start.39
  24.2 7.8 copy-start.38
  24.2 7.8 copy-start.36
  24.2 7.9 copy-start.37
  24.2 8.1 copy-start.13
  26.7 7.1 copy-start.40
  28.7 5.2 copy-start.14
  51.5 5.0 copy-start.6
  54.1 2.5 copy-start.24
  54.1 2.5 copy-start.29
  56.5 33.7 %copy-start.35 = (bf16[125,150]{0,1:T(8,128)(2,1)S(1)}, bf16[125,150]{0,1:T(8,128)(2,1)}, u32[]{:S(2)}) copy-start(bf16[125,150]{0,1:T(8,128)(2,1)} %constant.331) | copy-start | bytes 112504
  106.4 5.4 copy-start.3
  116.1 19.0 %copy-start.17 = (bf16[32,5,5,256]{3,2,1,0:T(8,128)(2,1)S(1)}, bf16[32,5,5,256]{3,2,1,0:T(8,128)(2,1)}, u32[]{:S(2)}) copy-start(bf16[32,5,5,256]{3,2,1,0:T(8,128)(2,1)} %get-tuple-element.61) | copy-start | bytes 1228804
  116.1 19.0 %copy-start.18 = (bf16[32,5,5,256]{3,2,1,0:T(8,128)(2,1)S(1)}, bf16[32,5,5,256]{3,2,1,0:T(8,128)(2,1)}, u32[]{:S(2)}) copy-start(bf16[32,5,5,256]{3,2,1,0:T(8,128)(2,1)} %get-tuple-element.62) | copy-start | bytes 1228804
  118.7 14.1 %collective-permute-start.2 = (bf16[16,5,5,256]{3,2,1,0:T(8,128)(2,1)S(1)}, bf16[16,5,5,256]{3,2,1,0:T(8,128)(2,1)S(1)}, u32[]{:S(2)}, u32[]{:S(2)}) collective-permute-start(bf16[16,5,5,256]{3,2,1,0:T(8,128)(2,1)S(1)} %bitcast.354), channel_id=1, source_target_pairs={{0,4},{4,8},{8,12},{12,16},{16,20},{20,24},{24,28},{28,0},{1,5},{5... | collective-permute-start | bytes 614408 | tf_op jit(solution)/shard_map/ppermute | solution.py:22
  118.8 16.2 %collective-permute-start.3 = (bf16[16,5,5,256]{3,2,1,0:T(8,128)(2,1)S(1)}, bf16[16,5,5,256]{3,2,1,0:T(8,128)(2,1)S(1)}, u32[]{:S(2)}, u32[]{:S(2)}) collective-permute-start(bf16[16,5,5,256]{3,2,1,0:T(8,128)(2,1)S(1)} %bitcast.357), channel_id=1, source_target_pairs={{4,0},{8,4},{12,8},{16,12},{20,16},{24,20},{28,24},{0,28},{5,1},{9... | collective-permute-start | bytes 614408 | tf_op jit(solution)/shard_map/ppermute | solution.py:24
  165.6 2.5 copy-start.30
  226.1 5.4 copy-start.4
  237.0 19.4 %copy-start.19 = (bf16[32,5,5,256]{3,2,1,0:T(8,128)(2,1)S(1)}, bf16[32,5,5,256]{3,2,1,0:T(8,128)(2,1)}, u32[]{:S(2)}) copy-start(bf16[32,5,5,256]{3,2,1,0:T(8,128)(2,1)} %get-tuple-element.53) | copy-start | bytes 1228804
  237.0 19.4 %copy-start.20 = (bf16[32,5,5,256]{3,2,1,0:T(8,128)(2,1)S(1)}, bf16[32,5,5,256]{3,2,1,0:T(8,128)(2,1)}, u32[]{:S(2)}) copy-start(bf16[32,5,5,256]{3,2,1,0:T(8,128)(2,1)} %get-tuple-element.54) | copy-start | bytes 1228804
  239.6 13.3 %collective-permute-start.4 = (bf16[16,5,5,256]{3,2,1,0:T(8,128)(2,1)S(1)}, bf16[16,5,5,256]{3,2,1,0:T(8,128)(2,1)S(1)}, u32[]{:S(2)}, u32[]{:S(2)}) collective-permute-start(bf16[16,5,5,256]{3,2,1,0:T(8,128)(2,1)S(1)} %bitcast.355), channel_id=1, source_target_pairs={{0,4},{4,8},{8,12},{12,16},{16,20},{20,24},{24,28},{28,0},{1,5},{5... | collective-permute-start | bytes 614408 | tf_op jit(solution)/shard_map/ppermute | solution.py:22
  239.9 16.5 %collective-permute-start.5 = (bf16[16,5,5,256]{3,2,1,0:T(8,128)(2,1)S(1)}, bf16[16,5,5,256]{3,2,1,0:T(8,128)(2,1)S(1)}, u32[]{:S(2)}, u32[]{:S(2)}) collective-permute-start(bf16[16,5,5,256]{3,2,1,0:T(8,128)(2,1)S(1)} %bitcast.358), channel_id=1, source_target_pairs={{4,0},{8,4},{12,8},{16,12},{20,16},{24,20},{28,24},{0,28},{5,1},{9... | collective-permute-start | bytes 614408 | tf_op jit(solution)/shard_map/ppermute | solution.py:24
  347.1 11.2 copy-start.2
  360.0 20.2 %copy-start.21 = (bf16[32,5,5,256]{3,2,1,0:T(8,128)(2,1)S(1)}, bf16[32,5,5,256]{3,2,1,0:T(8,128)(2,1)}, u32[]{:S(2)}) copy-start(bf16[32,5,5,256]{3,2,1,0:T(8,128)(2,1)} %get-tuple-element.45) | copy-start | bytes 1228804
  360.0 20.2 %copy-start.22 = (bf16[32,5,5,256]{3,2,1,0:T(8,128)(2,1)S(1)}, bf16[32,5,5,256]{3,2,1,0:T(8,128)(2,1)}, u32[]{:S(2)}) copy-start(bf16[32,5,5,256]{3,2,1,0:T(8,128)(2,1)} %get-tuple-element.46) | copy-start | bytes 1228804
  362.6 13.4 %collective-permute-start.6 = (bf16[16,5,5,256]{3,2,1,0:T(8,128)(2,1)S(1)}, bf16[16,5,5,256]{3,2,1,0:T(8,128)(2,1)S(1)}, u32[]{:S(2)}, u32[]{:S(2)}) collective-permute-start(bf16[16,5,5,256]{3,2,1,0:T(8,128)(2,1)S(1)} %bitcast.356), channel_id=1, source_target_pairs={{0,4},{4,8},{8,12},{12,16},{16,20},{20,24},{24,28},{28,0},{1,5},{5... | collective-permute-start | bytes 614408 | tf_op jit(solution)/shard_map/ppermute | solution.py:22
  362.7 17.5 %collective-permute-start.7 = (bf16[16,5,5,256]{3,2,1,0:T(8,128)(2,1)S(1)}, bf16[16,5,5,256]{3,2,1,0:T(8,128)(2,1)S(1)}, u32[]{:S(2)}, u32[]{:S(2)}) collective-permute-start(bf16[16,5,5,256]{3,2,1,0:T(8,128)(2,1)S(1)} %bitcast.359), channel_id=1, source_target_pairs={{4,0},{8,4},{12,8},{16,12},{20,16},{24,20},{28,24},{0,28},{5,1},{9... | collective-permute-start | bytes 614408 | tf_op jit(solution)/shard_map/ppermute | solution.py:24
  396.8 5.1 copy-start.7
  399.4 2.5 copy-start.28
  399.4 2.5 copy-start.32
  441.4 4.0 copy-start
  462.0 6.1 copy-start.34
  468.1 14.1 %collective-permute-start.8 = (bf16[16,5,5,256]{3,2,1,0:T(8,128)(2,1)}, bf16[16,5,5,256]{3,2,1,0:T(8,128)(2,1)}, u32[]{:S(2)}, u32[]{:S(2)}) collective-permute-start(bf16[16,5,5,256]{3,2,1,0:T(8,128)(2,1)} %bitcast.293), channel_id=1, source_target_pairs={{0,4},{4,8},{8,12},{12,16},{16,20},{20,24},{24,28},{28,0},{1,5},{5... | collective-permute-start | bytes 614408 | tf_op jit(solution)/shard_map/ppermute | solution.py:22
  468.9 17.8 %collective-permute-start.9 = (bf16[16,5,5,256]{3,2,1,0:T(8,128)(2,1)}, bf16[16,5,5,256]{3,2,1,0:T(8,128)(2,1)}, u32[]{:S(2)}, u32[]{:S(2)}) collective-permute-start(bf16[16,5,5,256]{3,2,1,0:T(8,128)(2,1)} %bitcast.292), channel_id=1, source_target_pairs={{4,0},{8,4},{12,8},{16,12},{20,16},{24,20},{28,24},{0,28},{5,1},{9... | collective-permute-start | bytes 614408 | tf_op jit(solution)/shard_map/ppermute | solution.py:24
  473.6 78.0 %all-to-all-start = ((bf16[4,1000,256]{2,1,0:T(8,128)(2,1)}), bf16[4,1000,256]{2,1,0:T(8,128)(2,1)}, u32[]{:S(2)}, u32[]{:S(2)}) async-start(bf16[4,1000,256]{2,1,0:T(8,128)(2,1)} %bitcast.78), calls=%async_computation | async-start | bytes 4096000 | tf_op jit(solution)/shard_map/all_to_all | solution.py:96
  504.5 5.0 copy-start.10
  507.1 2.5 copy-start.23
  507.1 2.5 copy-start.25
  551.6 28.7 %all-to-all-start.2 = ((bf16[4,1000,256]{2,1,0:T(8,128)(2,1)}), bf16[4,1000,256]{2,1,0:T(8,128)(2,1)S(1)}, u32[]{:S(2)}, u32[]{:S(2)}) async-start(bf16[4,1000,256]{2,1,0:T(8,128)(2,1)} %convert_element_type.99), calls=%async_computation.2 | async-start | bytes 4096000 | tf_op jit(solution)/shard_map/all_to_all | solution.py:97
  555.2 209.8 %all-reduce.4.cloned.1.call-start = ((), (), s32[]{:S(2)}) async-start(), calls=%async_computation.3 | async-start | bytes 16777216 | tf_op jit(solution)/shard_map/psum | solution.py:106
  1093.5 3.2 copy-start.8
  1111.7 4.2 copy-start.33
  1119.8 28.8 %all-to-all-start.1 = ((bf16[1000,4,256]{2,0,1:T(8,128)(2,1)}), bf16[1000,4,256]{2,0,1:T(8,128)(2,1)S(1)}, u32[]{:S(2)}, u32[]{:S(2)}) async-start(bf16[1000,4,256]{2,0,1:T(8,128)(2,1)} %bitcast.309), calls=%async_computation.1 | async-start | bytes 4096000 | tf_op jit(solution)/shard_map/all_to_all | solution.py:120
  1123.4 6.2 copy-start.12
  (7 other events, 15.2 us)
Sparse Core Ops, SparseCore 0:
  589.6 175.3 all-reduce.3
where the time goes:
time: 1170 us; the launch traced here: 1160 us
  local copies, waits for them, and re-layouts  425 us (36%)
  other arithmetic  328 us (28%)
  waiting for transfers between devices  241 us (21%)
  matrix products  102 us (9%)
  starting transfers between devices  37.3 us (3%)
  between operations  23.3 us (2%)
    concatenate x5, local copies, waits for them, and re-layouts, apply_operator(): stacked = jnp.concatenate(pieces, axis=1)  177 us
    another operation x31, other arithmetic, per_device(): lower = jnp.linalg.cholesky(margin)  173 us
    psum x1, waiting for transfers between devices, per_device(): lax.psum((margin_part, cross_part), ('domain', 'band'))  172 us
    another operation x3, other arithmetic, per_device(): jax.scipy.linalg.solve_triangular(lower, jnp.eye(margin.shape[0], dtype=j...  83.9 us
    gather x30, local copies, waits for them, and re-layouts, apply_operator(): nearby = jnp.take(table, neighbours[:, direction], axis=0)  59.2 us
    reshape x30, local copies, waits for them, and re-layouts, apply_operator(): pieces.append(nearby.reshape(cell_count, 25, columns))  31.3 us
    dot_general x5, matrix products, apply_operator(): jnp.einsum('mn,cnb->cmb', combined, stacked, preferred_element_type=jnp.f...  30.3 us
    squeeze x19, local copies, waits for them, and re-layouts, face_view(): lax.index_in_dim(field, 4 * (direction % 2), 1 + direction // 2, keepdims...  25.7 us
  transfers between devices with their start and end apart: 14, of which 11 were waited for; matrix products, arithmetic and copies ran while one was open for 9% of the time, Pallas kernels for 0%

commit v1 on v0

v1 whole, which is shorter than its diff:
```python
import functools

import jax
import jax.numpy as jnp
import numpy as np
from jax import lax
from jax.experimental import pallas as pl
from jax.experimental.pallas import tpu as pltpu
from jax.sharding import PartitionSpec as P

NPC = 125
ROWS = 128
FACE = 32
GROUP = 4
BLOCK = 128
penalty = 0.5
highest = lax.Precision.HIGHEST
MESH = pl.DeviceIdType.MESH


def face_table():
    incidence = np.zeros((ROWS, 6 * FACE), np.float32)
    for direction in range(6):
        axis_index = direction // 2
        level = 4 * (direction % 2)
        for first in range(5):
            for second in range(5):
                others = [first, second]
                coords = others[:axis_index] + [level] + others[axis_index:]
                node = 25 * coords[0] + 5 * coords[1] + coords[2]
                incidence[node, FACE * direction + 5 * first + second] = 1.0
    return incidence


def chain_kernel(steps, plain, count, half_cells, *refs):
    nb_ref, coef_ref, start_ref, weight_ref, comb_ref, pick_ref, out_ref = refs[:7]
    rest = list(refs[7:])
    fields = [start_ref] + rest[: steps - 1] + [out_ref]
    rest = rest[steps - 1 :]
    faces, below, above = rest[:steps], rest[steps : 2 * steps], rest[2 * steps : 3 * steps]
    send_sem, recv_sem = rest[3 * steps :]
    me = lax.axis_index("domain")
    up, down = lax.rem(me + 1, count), lax.rem(me + count - 1, count)

    barrier = pltpu.get_barrier_semaphore()
    for other in (down, up):
        pl.semaphore_signal(barrier, inc=1, device_id={"domain": other}, device_id_type=MESH)
    pl.semaphore_wait(barrier, 2)

    def copy_of(step, part):
        return pltpu.make_async_remote_copy(
            src_ref=faces[step].at[4 + part, pl.ds(half_cells * part, half_cells)],
            dst_ref=(below if part else above)[step],
            send_sem=send_sem.at[step, part],
            recv_sem=recv_sem.at[step, part],
            device_id={"domain": up if part else down},
            device_id_type=MESH,
        )

    def store_faces(step, cell, value):
        picked = jnp.dot(pick_ref[...], value, preferred_element_type=jnp.float32)
        picked = picked.astype(jnp.bfloat16)
        for d in range(6):
            faces[step][d, cell] = picked[FACE * d : FACE * (d + 1)]

    center = coef_ref[0]

    def work(step, part):
        scale = 1.0 if plain else coef_ref[1 if step == 0 else 2]
        shift = 0.0 if plain else center
        now, later = fields[step], fields[step + 1]
        before = fields[step - 1] if step > 0 else None

        def body(index, carry):
            for inner in range(GROUP):
                cell = half_cells * part + index * GROUP + inner
                value = now[cell]
                pieces = [value]
                for d in range(6):
                    slot = nb_ref[cell, d]
                    if d == 4 and part == 0:
                        pieces.append(below[step][lax.rem(slot, half_cells)])
                    elif d == 5 and part == 1:
                        pieces.append(above[step][lax.rem(slot, half_cells)])
                    else:
                        pieces.append(faces[step][d ^ 1, slot])
                stacked = jnp.concatenate(pieces, axis=0)
                image = jnp.dot(comb_ref[...], stacked, preferred_element_type=jnp.float32)
                wide = value.astype(jnp.float32)
                if plain:
                    image = image + weight_ref[cell] * wide
                else:
                    image = image * scale + ((weight_ref[cell] - shift) * scale) * wide
                if before is not None:
                    image = image - before[cell].astype(jnp.float32)
                result = image.astype(jnp.bfloat16)
                later[cell] = result
                if step + 1 < steps:
                    store_faces(step + 1, cell, result)
            return carry

        lax.fori_loop(0, half_cells // GROUP, body, 0)

    def first_faces(part):
        def body(index, carry):
            for inner in range(GROUP):
                cell = half_cells * part + index * GROUP + inner
                store_faces(0, cell, start_ref[cell])
            return carry

        lax.fori_loop(0, half_cells // GROUP, body, 0)

    for part in (0, 1):
        first_faces(part)
        copy_of(0, part).start()
    order = (1, 0)
    for step in range(steps):
        for part in order:
            copy_of(step, 1 - part).wait_recv()
            work(step, part)
            if step + 1 < steps:
                copy_of(step + 1, part).start()
        order = order[::-1]
    for step in range(steps):
        for part in (0, 1):
            copy_of(step, part).wait_send()


def chain(start, neighbours, coefs, weight, comb, pick, steps, plain, ident):
    count = lax.axis_size("domain")
    cells, _, columns = start.shape
    half_cells = cells // 2
    vmem = pl.BlockSpec(memory_space=pltpu.VMEM)
    smem = pl.BlockSpec(memory_space=pltpu.SMEM)
    field = pltpu.VMEM(start.shape, jnp.bfloat16)
    rim = pltpu.VMEM((half_cells, FACE, columns), jnp.bfloat16)
    return pl.pallas_call(
        functools.partial(chain_kernel, steps, plain, count, half_cells),
        out_shape=jax.ShapeDtypeStruct(start.shape, jnp.bfloat16),
        in_specs=[smem, smem, vmem, vmem, vmem, vmem],
        out_specs=vmem,
        scratch_shapes=[field] * (steps - 1)
        + [pltpu.VMEM((6, cells, FACE, columns), jnp.bfloat16)] * steps
        + [rim] * (2 * steps)
        + [pltpu.SemaphoreType.DMA((steps, 2)), pltpu.SemaphoreType.DMA((steps, 2))],
        compiler_params=pltpu.CompilerParams(
            collective_id=ident, has_side_effects=True, vmem_limit_bytes=48 * 2**20
        ),
        cost_estimate=pl.CostEstimate(
            flops=steps * cells * 2 * columns * ROWS * 512,
            bytes_accessed=steps * 16 * 2**20,
            transcendentals=0,
        ),
        name="chain" if not plain else "image",
    )(neighbours, coefs, start, weight, comb, pick)


def factor_inverse(block):
    lanes = lax.broadcasted_iota(jnp.int32, (8, BLOCK), 1)
    subs = lax.broadcasted_iota(jnp.int32, (8, BLOCK), 0)
    tiles = [block[8 * t : 8 * t + 8] for t in range(BLOCK // 8)]
    done = [jnp.zeros((8, BLOCK), jnp.float32) for _ in tiles]
    for j in range(BLOCK):
        at, within = divmod(j, 8)
        row = jnp.broadcast_to(tiles[at][within : within + 1], (8, BLOCK))
        pivot = jnp.broadcast_to(row[:, j : j + 1], (8, BLOCK))
        here = lanes == j
        unit = jnp.where(here, 1.0, row)
        scaled = unit * (1.0 / pivot)
        final = jnp.where(lanes <= j, unit, 0.0) * lax.rsqrt(pivot)
        done[at] = jnp.where(subs == within, final, done[at])
        for t in range(at, BLOCK // 8):
            if t == at and within == 7:
                continue
            tile = tiles[t]
            column = jnp.broadcast_to(tile[:, j : j + 1], (8, BLOCK))
            fresh = jnp.where(here, 0.0, tile) - column * scaled
            tiles[t] = jnp.where(subs > within, fresh, tile) if t == at else fresh
    return jnp.concatenate(done, axis=0)


def inverse_kernel(source_ref, out_ref, row_ref):
    size = source_ref.shape[0]
    blocks = size // BLOCK
    out_ref[...] = source_ref[...]
    rows_of = lax.broadcasted_iota(jnp.int32, (BLOCK, BLOCK), 0)
    lanes_of = lax.broadcasted_iota(jnp.int32, (BLOCK, BLOCK), 1)
    eye = (rows_of == lanes_of).astype(jnp.float32)
    column_ids = lax.broadcasted_iota(jnp.int32, (BLOCK, size), 1)

    def step(k, carry):
        base = pl.multiple_of(k * BLOCK, BLOCK)
        own = pl.ds(base, BLOCK)
        small = factor_inverse(out_ref[own, own])
        out_ref[own, own] = eye
        row_ref[...] = jnp.dot(
            small, out_ref[own, :], precision=highest, preferred_element_type=jnp.float32
        )
        out_ref[own, :] = jnp.where(column_ids < base + BLOCK, row_ref[...], 0.0)

        def update(i, inner):
            low = pl.ds(pl.multiple_of(i * BLOCK, BLOCK), BLOCK)
            out_ref[low, own] = jnp.zeros((BLOCK, BLOCK), jnp.float32)
            out_ref[low, :] = out_ref[low, :] - lax.dot_general(
                row_ref[:, low],
                row_ref[...],
                (((0,), (0,)), ((), ())),
                precision=highest,
                preferred_element_type=jnp.float32,
            )
            return inner

        return lax.fori_loop(k + 1, blocks, update, carry)

    lax.fori_loop(0, blocks, step, 0)


def cholesky_inverse(margin):
    size = margin.shape[0]
    return pl.pallas_call(
        inverse_kernel,
        out_shape=jax.ShapeDtypeStruct(margin.shape, jnp.float32),
        in_specs=[pl.BlockSpec(memory_space=pltpu.VMEM)],
        out_specs=pl.BlockSpec(memory_space=pltpu.VMEM),
        scratch_shapes=[pltpu.VMEM((BLOCK, size), jnp.float32)],
        compiler_params=pltpu.CompilerParams(vmem_limit_bytes=40 * 2**20),
        cost_estimate=pl.CostEstimate(
            flops=40 * size**3, bytes_accessed=8 * size * size, transcendentals=size
        ),
        name="cholesky_inverse",
    )(margin)


def per_device(wavefunctions, potential, cell_matrix, neighbours, window):
    cells = neighbours.shape[0]
    nodes, columns = wavefunctions.shape
    wide = cell_matrix.astype(jnp.float32)
    stiffness = ((wide + wide.T) * 0.5).astype(jnp.bfloat16)
    table = face_table()
    pad = ROWS - NPC
    comb = jnp.concatenate(
        [jnp.pad(stiffness, ((0, pad), (0, pad))), jnp.asarray(-penalty * table, jnp.bfloat16)],
        axis=1,
    )
    pick = jnp.asarray(table.T, jnp.bfloat16)
    weight = (
        jnp.pad(potential.reshape(cells, NPC), ((0, 0), (0, pad)))
        + penalty * jnp.asarray(table.sum(axis=1))[None, :]
    )[:, :, None]
    center = (window[0] + window[1]) * 0.5
    half = (window[1] - window[0]) * 0.5
    coefs = jnp.stack([center, 1.0 / half, 2.0 / half])
    start = jnp.pad(wavefunctions.reshape(cells, NPC, columns), ((0, 0), (0, pad), (0, 0)))
    common = (neighbours, coefs, weight, comb, pick)
    last = chain(start, *common, 4, False, 0)
    gathered = lax.all_gather(last.reshape(cells * ROWS, columns), "band", axis=0)
    image = chain(last, *common, 1, True, 1).reshape(cells * ROWS, columns)
    last = last.reshape(cells * ROWS, columns)
    bands = gathered.shape[0]
    size = bands * columns

    margin_part = jnp.einsum(
        "bni,nj->bij", gathered, last, preferred_element_type=jnp.float32
    ).reshape(size, columns)
    cross_part = jnp.einsum(
        "bni,nj->bij", gathered, image, preferred_element_type=jnp.float32
    ).reshape(size, columns)
    total_rows = nodes * lax.axis_size("domain")
    margin_cols = lax.psum(margin_part, "domain")
    cross_cols = lax.psum(cross_part, "domain")
    margin = lax.all_gather(margin_cols.T / total_rows, "band", axis=0, tiled=True)
    cross = lax.all_gather(cross_cols / total_rows, "band", axis=0)
    inverse = cholesky_inverse(margin)
    mine = lax.dynamic_slice_in_dim(inverse, lax.axis_index("band") * columns, columns, 0)
    filtered = jnp.einsum(
        "bnj,kbj->nk",
        gathered,
        mine.astype(jnp.bfloat16).reshape(columns, bands, columns),
        preferred_element_type=jnp.float32,
    ).astype(jnp.bfloat16)
    filtered = filtered.reshape(cells, ROWS, columns)[:, :NPC].reshape(nodes, columns)
    left = jnp.einsum(
        "ik,bkj->ibj", mine, cross, precision=highest, preferred_element_type=jnp.float32
    ).reshape(columns, size)
    projected = lax.dot_general(
        left,
        inverse,
        (((1,), (1,)), ((), ())),
        precision=highest,
        preferred_element_type=jnp.float32,
    )
    return (filtered, projected)


def solution(mesh):
    placed = (P("domain", "band"), P("domain"), P(), P("domain", None), P())
    return jax.shard_map(
        per_device,
        mesh=mesh,
        in_specs=placed,
        out_specs=(P("domain", "band"), P("band", None)),
        check_vma=False,
    )
```

time: 1170 us -> 508 us (0.43); the launches traced: 1160 us -> 507 us
  local copies, waits for them, and re-layouts: 425 us -> 25.4 us
  other arithmetic: 328 us -> 5.48 us
  Pallas kernels: 0 us -> 247 us
  matrix products: 102 us -> 28.4 us
  waiting for transfers between devices: 241 us -> 184 us
  starting transfers between devices: 37.3 us -> 0.34 us
    another operation x34 -> x1, other arithmetic: 257 us -> 0.08 us  [per_device(): coefs = jnp.stack([center, 1.0 / half, 2.0 / half])]
    pallas_call x0 -> x3, Pallas kernels: none -> 247 us  [the longest x1 160 us: cholesky_inverse(): pl.pallas_call(inverse_kernel, out_shape=jax.ShapeDtypeStruct(margin.shap...]
    concatenate x5 -> x0, local copies, waits for them, and re-layouts: 177 us -> none  [apply_operator(): stacked = jnp.concatenate(pieces, axis=1)]
    all_gather x0 -> x3, waiting for transfers between devices: none -> 81.9 us  [the longest x1 50.1 us: per_device(): lax.all_gather(last.reshape(cells * ROWS, columns), 'band', axis=0)]
    reshape x45 -> x3, local copies, waits for them, and re-layouts: 77.6 us -> 4.3 us  [the longest x1 1.86 us: per_device(): wavefunctions.reshape(cells, NPC, columns)]
    psum x1, waiting for transfers between devices: 172 us -> 102 us  [per_device(): margin_cols = lax.psum(margin_part, 'domain')]
    gather x30 -> x0, local copies, waits for them, and re-layouts: 59.2 us -> none  [apply_operator(): nearby = jnp.take(table, neighbours[:, direction], axis=0)]
    another operation x29 -> x0, matrix products: 45.5 us -> none  [the longest x14 23.3 us: per_device(): lower = jnp.linalg.cholesky(margin)]
  transfers between devices with their start and end apart: 14 -> 4, of which waited for: 11 -> 3; matrix products, arithmetic and copies ran while one was open for 9% -> 0% of each run, Pallas kernels for 0% -> 35%
where the time goes in v1:
time: 508 us; the launch traced here: 507 us
  Pallas kernels  247 us (49%)
  waiting for transfers between devices  184 us (36%)
  matrix products  28.4 us (6%)
  local copies, waits for them, and re-layouts  25.4 us (5%)
  between operations  16.6 us (3%)
  other arithmetic  5.48 us (1%)
    pallas_call x1, Pallas kernels, cholesky_inverse(): pl.pallas_call(inverse_kernel, out_shape=jax.ShapeDtypeStruct(margin.shap...  160 us
    psum x1, waiting for transfers between devices, per_device(): margin_cols = lax.psum(margin_part, 'domain')  102 us
    pallas_call x2, Pallas kernels, chain(): pl.pallas_call(functools.partial(chain_kernel, steps, plain, count, half_...  87 us
    all_gather x1, waiting for transfers between devices, per_device(): lax.all_gather(last.reshape(cells * ROWS, columns), 'band', axis=0)  50.1 us
    all_gather x1, waiting for transfers between devices, per_device(): lax.all_gather(margin_cols.T / total_rows, 'band', axis=0, tiled=True)  31.8 us
    all_gather x1, local copies, waits for them, and re-layouts, per_device(): lax.all_gather(last.reshape(cells * ROWS, columns), 'band', axis=0)  11.5 us
  transfers between devices with their start and end apart: 4, of which 3 were waited for; matrix products, arithmetic and copies ran while one was open for 0% of the time, Pallas kernels for 35%

profile of v1, /device:TPU:0, one launch (start us, length us, event | category | flops | bytes accessed | tf_op | source)
XLA Modules:
  0.0 507.1 jit_solution(8594027844119975616)
XLA Ops:
  7.2 0.0 copy-start.6
  7.2 0.0 all-gather.5.cloned.1.call-start
  7.2 1.3 fusion.13
  11.2 0.9 copy.29
  12.1 0.1 copy.30
  12.2 0.8 reshape.48
  13.1 0.7 add_bitcast_fusion
  13.7 2.0 copy.32.refs_3_
  15.8 0.8 copy.31.refs_0_
  16.5 0.0 copy-start.2
  16.5 1.9 reshape.47
  18.4 0.0 copy-done.6
  18.4 0.2 pad.12.refs_2_
  18.6 0.1 pad_maximum_fusion.refs_1_
  18.7 0.0 copy-done.2
  18.7 67.2 %chain.1.refs_2_ = bf16[32,128,256]{2,1,0:T(8,128)(2,1)} custom-call(s32[32,6]{1,0:T(8,128)S(1)} %copy.31.refs_0_, f32[3]{0:T(128)S(1)} %pad_maximum_fusion.refs_1_, bf16[32,128,256]{2,1,0:T(8,128)(2,1)S(1)} %pad.12.refs_2_, f32[32,128,1]{2,1,0:T(8,128)} %copy.32.refs_3_, bf16[128,320]{1,0:T(8,128)(2,1)S(1)} %fusion.9.refs_4_, bf16[192,128]{1,0:T(8,128)(2,1)S(1)} %copy-done.2), custom_call_target="tpu_custom_call" | custom-call | flops 4294967296 | bytes 67108864 | tf_op jit(solution)/shard_map/chain/pallas_call | solution.py:137
  85.9 0.0 all-gather.5.cloned.1.call-update
  85.9 0.0 all-reduce.6.cloned.1.call-start
  86.0 19.8 %image.1 = bf16[32,128,256]{2,1,0:T(8,128)(2,1)S(1)} custom-call(s32[32,6]{1,0:T(8,128)S(1)} %copy.31.refs_0_, f32[3]{0:T(128)S(1)} %pad_maximum_fusion.refs_1_, bf16[32,128,256]{2,1,0:T(8,128)(2,1)} %chain.1.refs_2_, f32[32,128,1]{2,1,0:T(8,128)} %copy.32.refs_3_, bf16[128,320]{1,0:T(8,128)(2,1)S(1)} %fusion.9.refs_4_, bf16[192,128]{1,0:T(8,128)(2,1)S(1)} %copy-done.2), custom_call_target="tpu_custom_call" | custom-call | flops 1073741824 | bytes 16777216 | tf_op jit(solution)/shard_map/image/pallas_call | solution.py:137
  105.8 50.1 %all-gather.5.cloned.1.call-done = bf16[4,4096,256]{2,1,0:T(8,128)(2,1)} async-done(((bf16[1,4096,256]{2,1,0:T(8,128)(2,1)}), bf16[4,4096,256]{2,1,0:T(8,128)(2,1)}) %all-gather.5.cloned.1.call-update) | async-done | bytes 8388624 | tf_op jit(solution)/shard_map/all_gather | solution.py:256
  155.9 11.5 %copy.33 = bf16[4,4096,256]{1,2,0:T(8,128)(2,1)} copy(bf16[4,4096,256]{2,1,0:T(8,128)(2,1)} %all-gather.5.cloned.1.call-done) | data formatting | bytes 16777216 | tf_op jit(solution)/shard_map/all_gather | solution.py:256
  167.4 0.0 copy-start.5
  167.4 6.9 %fusion.15 = f32[1024,256]{0,1:T(8,128)} fusion(bf16[1024,4096]{1,0:T(8,128)(2,1)} %bitcast.42, bf16[4096,256]{1,0:T(8,128)(2,1)S(1)} %bitcast.41), kind=kOutput, calls=%fused_computation.23 | convolution fusion | flops 2147483648 | bytes 11534336 | tf_op jit(solution)/shard_map/bni,nj->bij/dot_general | solution.py:265
  174.3 0.0 copy-done.5
  174.3 5.0 fusion.14
  179.3 0.0 all-reduce.6.cloned.1.call-update
  179.3 0.0 all-gather.7.cloned.1.call-start
  179.4 102.3 %all-reduce.6.cloned.1.call-done = (f32[1024,256]{0,1:T(8,128)}, f32[1024,256]{0,1:T(8,128)}) async-done(((f32[1024,256]{0,1:T(8,128)}, f32[1024,256]{0,1:T(8,128)}), (f32[1024,256]{0,1:T(8,128)}, f32[1024,256]{0,1:T(8,128)})) %all-reduce.6.cloned.1.call-update) | async-done | bytes 2097168 | tf_op jit(solution)/shard_map/psum | solution.py:269
  281.6 2.3 multiply_bitcast_fusion
  284.0 0.0 all-gather.7.cloned.1.call-update
  284.0 0.2 all-gather.9.cloned.1.call-start
  284.2 2.3 broadcast_multiply_fusion
  286.6 0.0 all-gather.9.cloned.1.call-update
  286.6 31.8 %all-gather.7.cloned.1.call-done.source_ref = f32[1024,1024]{1,0:T(8,128)} async-done(((f32[256,1024]{1,0:T(8,128)}), f32[1024,1024]{1,0:T(8,128)}) %all-gather.7.cloned.1.call-update) | async-done | bytes 4194320 | tf_op jit(solution)/shard_map/all_gather | solution.py:271
  318.4 2.2 copy-done.3
  320.6 159.7 %cholesky_inverse.1 = f32[1024,1024]{1,0:T(8,128)S(1)} custom-call(f32[1024,1024]{1,0:T(8,128)S(1)} %copy-done.3), custom_call_target="tpu_custom_call" | custom-call | flops 42949672960 | bytes 8388608 | tf_op jit(solution)/shard_map/cholesky_inverse/pallas_call | solution.py:220
  480.3 0.0 copy-start
  480.3 2.0 copy-done
  482.2 0.1 dynamic-slice_convert_fusion
  482.3 0.0 all-gather.9.cloned.1.call-done
  482.4 0.0 copy-start.1
  482.4 0.0 copy-start.4
  482.4 6.1 %fusion.1 = f32[256,4,256]{0,2,1:T(8,128)S(1)} fusion(f32[32,4,8,1024]{3,2,1,0:T(8,128)} %bitcast.44, f32[1024,1024]{1,0:T(8,128)} %copy-done, s32[]{:T(128)S(6)} %select_n.3), kind=kOutput, calls=%fused_computation.2 | convolution fusion | flops 3221225472 | bytes 6291460 | tf_op jit(solution)/shard_map/ik,bkj->ibj/dot_general | solution.py:282
  488.5 0.0 copy-done.1
  488.5 8.0 %fusion.16 = f32[256,1024]{1,0:T(8,128)} fusion(f32[256,1024]{0,1:T(8,128)S(1)} %bitcast.45, f32[1024,1024]{1,0:T(8,128)S(1)} %copy-done.1), kind=kOutput, calls=%fused_computation.24 | convolution fusion | flops 3221225472 | bytes 6291456 | tf_op jit(solution)/shard_map/dot_general | solution.py:285
  496.6 0.0 copy-done.4
  496.6 2.4 fusion
  499.0 1.6 reshape.52
  (3 shorter events, 0.0 us)
Async XLA Ops:
  7.2 11.2 %copy-start.6 = (bf16[128,192]{1,0:T(8,128)(2,1)S(1)}, bf16[128,192]{1,0:T(8,128)(2,1)}, u32[]{:S(2)}) copy-start(bf16[128,192]{1,0:T(8,128)(2,1)} %constant.38.clone) | copy-start | bytes 147460
  7.2 148.7 %all-gather.5.cloned.1.call-start = ((), (), s32[]{:S(2)}) async-start(), calls=%async_computation | async-start | bytes 10485760 | tf_op jit(solution)/shard_map/all_gather | solution.py:256
  16.5 2.2 copy-start.2
  85.9 195.7 %all-reduce.6.cloned.1.call-start = ((), (), s32[]{:S(2)}) async-start(), calls=%async_computation.3 | async-start | bytes 4194304 | tf_op jit(solution)/shard_map/psum | solution.py:269
  167.4 6.9 %copy-start.5 = (bf16[4,4096,256]{1,2,0:T(8,128)(2,1)S(1)}, bf16[4,4096,256]{1,2,0:T(8,128)(2,1)}, u32[]{:S(2)}) copy-start(bf16[4,4096,256]{1,2,0:T(8,128)(2,1)} %copy.33) | copy-start | bytes 25165828
  179.3 139.1 %all-gather.7.cloned.1.call-start = ((), (), s32[]{:S(2)}) async-start(), calls=%async_computation.1 | async-start | bytes 5242880 | tf_op jit(solution)/shard_map/all_gather | solution.py:271
  284.0 198.3 %all-gather.9.cloned.1.call-start = ((), (), s32[]{:S(2)}) async-start(), calls=%async_computation.2 | async-start | bytes 5242880 | tf_op jit(solution)/shard_map/all_gather | solution.py:272
  318.4 2.2 copy-start.3
  480.3 2.0 copy-start
  482.4 6.2 %copy-start.1 = (f32[1024,1024]{1,0:T(8,128)S(1)}, f32[1024,1024]{1,0:T(8,128)}, u32[]{:S(2)}) copy-start(f32[1024,1024]{1,0:T(8,128)} %copy-done) | copy-start | bytes 12582916
  482.4 14.2 %copy-start.4 = (bf16[4,4096,256]{2,1,0:T(8,128)(2,1)S(1)}, bf16[4,4096,256]{2,1,0:T(8,128)(2,1)}, u32[]{:S(2)}) copy-start(bf16[4,4096,256]{2,1,0:T(8,128)(2,1)} %all-gather.5.cloned.1.call-done) | copy-start | bytes 25165828
Sparse Core Ops, SparseCore 0:
  86.0 69.7 all-gather.4
  179.4 102.1 all-reduce.5
  284.1 34.2 all-gather.6
  320.4 34.5 all-gather.8

commit v2 on v1

--- a/solution.py
+++ b/solution.py
@@ -13,6 +13,7 @@
 FACE = 32
 GROUP = 4
 BLOCK = 128
+PIVOTS = 4
 penalty = 0.5
 highest = lax.Precision.HIGHEST
 MESH = pl.DeviceIdType.MESH
@@ -160,26 +161,46 @@
     subs = lax.broadcasted_iota(jnp.int32, (8, BLOCK), 0)
     tiles = [block[8 * t : 8 * t + 8] for t in range(BLOCK // 8)]
     done = [jnp.zeros((8, BLOCK), jnp.float32) for _ in tiles]
-    for j in range(BLOCK):
+    for j in range(0, BLOCK, PIVOTS):
         at, within = divmod(j, 8)
-        row = jnp.broadcast_to(tiles[at][within : within + 1], (8, BLOCK))
-        pivot = jnp.broadcast_to(row[:, j : j + 1], (8, BLOCK))
-        here = lanes == j
-        unit = jnp.where(here, 1.0, row)
-        scaled = unit * (1.0 / pivot)
-        final = jnp.where(lanes <= j, unit, 0.0) * lax.rsqrt(pivot)
-        done[at] = jnp.where(subs == within, final, done[at])
+        own = range(PIVOTS)
+        raw = [
+            jnp.broadcast_to(tiles[at][within + s : within + s + 1], (8, BLOCK)) for s in own
+        ]
+        entry = [
+            [jnp.broadcast_to(raw[s][:, j + t : j + t + 1], (8, BLOCK)) for t in range(s + 1)]
+            for s in own
+        ]
+        here = (lanes >= j) & (lanes < j + PIVOTS)
+        rows = [jnp.where(lanes == j + s, 1.0, jnp.where(here, 0.0, raw[s])) for s in own]
+        inv = []
+        ratio = [[None] * PIVOTS for _ in own]
+        for t in own:
+            inv.append(1.0 / entry[t][t])
+            final = jnp.where(lanes <= j + t, rows[t], 0.0) * lax.rsqrt(entry[t][t])
+            done[at] = jnp.where(subs == within + t, final, done[at])
+            for s in range(t + 1, PIVOTS):
+                ratio[s][t] = entry[s][t] * inv[t]
+            for s in range(t + 1, PIVOTS):
+                for q in range(t + 1, s + 1):
+                    entry[s][q] = entry[s][q] - ratio[s][t] * entry[q][t]
+                rows[s] = rows[s] - ratio[s][t] * rows[t]
+        solved = [rows[t] * inv[t] for t in own]
+        for t in reversed(own):
+            for s in range(t):
+                solved[s] = solved[s] - ratio[t][s] * solved[t]
         for t in range(at, BLOCK // 8):
-            if t == at and within == 7:
+            if t == at and within + PIVOTS == 8:
                 continue
             tile = tiles[t]
-            column = jnp.broadcast_to(tile[:, j : j + 1], (8, BLOCK))
-            fresh = jnp.where(here, 0.0, tile) - column * scaled
-            tiles[t] = jnp.where(subs > within, fresh, tile) if t == at else fresh
+            fresh = jnp.where(here, 0.0, tile)
+            for s in own:
+                fresh = fresh - jnp.broadcast_to(tile[:, j + s : j + s + 1], (8, BLOCK)) * solved[s]
+            tiles[t] = jnp.where(subs >= within + PIVOTS, fresh, tile) if t == at else fresh
     return jnp.concatenate(done, axis=0)
 
 
-def inverse_kernel(source_ref, out_ref, row_ref):
+def inverse_kernel(first, last, source_ref, out_ref, row_ref):
     size = source_ref.shape[0]
     blocks = size // BLOCK
     out_ref[...] = source_ref[...]
@@ -212,20 +233,20 @@
 
         return lax.fori_loop(k + 1, blocks, update, carry)
 
-    lax.fori_loop(0, blocks, step, 0)
-
-
-def cholesky_inverse(margin):
+    lax.fori_loop(first, last, step, 0)
+
+
+def cholesky_inverse(margin, first, last):
     size = margin.shape[0]
     return pl.pallas_call(
-        inverse_kernel,
+        functools.partial(inverse_kernel, first, last),
         out_shape=jax.ShapeDtypeStruct(margin.shape, jnp.float32),
         in_specs=[pl.BlockSpec(memory_space=pltpu.VMEM)],
         out_specs=pl.BlockSpec(memory_space=pltpu.VMEM),
         scratch_shapes=[pltpu.VMEM((BLOCK, size), jnp.float32)],
         compiler_params=pltpu.CompilerParams(vmem_limit_bytes=40 * 2**20),
         cost_estimate=pl.CostEstimate(
-            flops=40 * size**3, bytes_accessed=8 * size * size, transcendentals=size
+            flops=75 * size**3, bytes_accessed=8 * size * size, transcendentals=size
         ),
         name="cholesky_inverse",
     )(margin)
@@ -259,18 +280,27 @@
     bands = gathered.shape[0]
     size = bands * columns
 
-    margin_part = jnp.einsum(
-        "bni,nj->bij", gathered, last, preferred_element_type=jnp.float32
-    ).reshape(size, columns)
+    total_rows = nodes * lax.axis_size("domain")
+    contract = (((0,), (0,)), ((), ()))
+    margin_part = jnp.concatenate(
+        [
+            lax.dot_general(last, gathered[b], contract, preferred_element_type=jnp.float32)
+            for b in range(bands)
+        ],
+        axis=1,
+    )
+    margin_rows = lax.psum(margin_part, "domain")
+    margin = lax.all_gather(margin_rows / total_rows, "band", axis=0, tiled=True)
+    image, margin = lax.optimization_barrier((image, margin))
     cross_part = jnp.einsum(
         "bni,nj->bij", gathered, image, preferred_element_type=jnp.float32
     ).reshape(size, columns)
-    total_rows = nodes * lax.axis_size("domain")
-    margin_cols = lax.psum(margin_part, "domain")
     cross_cols = lax.psum(cross_part, "domain")
-    margin = lax.all_gather(margin_cols.T / total_rows, "band", axis=0, tiled=True)
+    blocks = size // BLOCK
+    begun = cholesky_inverse(margin, 0, blocks // 2)
+    cross_cols, begun = lax.optimization_barrier((cross_cols, begun))
     cross = lax.all_gather(cross_cols / total_rows, "band", axis=0)
-    inverse = cholesky_inverse(margin)
+    inverse = cholesky_inverse(begun, blocks // 2, blocks)
     mine = lax.dynamic_slice_in_dim(inverse, lax.axis_index("band") * columns, columns, 0)
     filtered = jnp.einsum(
         "bnj,kbj->nk",

time: 508 us -> 429 us (0.84)
  Pallas kernels: 247 us -> 160 us
  local copies, waits for them, and re-layouts: 25.4 us -> 15.2 us
  matrix products: 28.4 us -> 37.7 us
  waiting for transfers between devices: 184 us -> 193 us
    pallas_call x1 -> x2, Pallas kernels: 160 us -> 73.6 us  [cholesky_inverse(): pl.pallas_call(functools.partial(inverse_kernel, first, last), out_shape=...]
    all_gather x1, waiting for transfers between devices: 50.1 us -> 67.3 us  [per_device(): lax.all_gather(last.reshape(cells * ROWS, columns), 'band', axis=0)]
    all_gather x1, waiting for transfers between devices: 31.8 us -> 15.2 us  [per_device(): lax.all_gather(margin_rows / total_rows, 'band', axis=0, tiled=True)]
    all_gather x1 -> x0, local copies, waits for them, and re-layouts: 11.5 us -> none  [per_device(): lax.all_gather(last.reshape(cells * ROWS, columns), 'band', axis=0)]
    psum x1 -> x2, waiting for transfers between devices: 102 us -> 110 us  [the longest x1 78.1 us: per_device(): margin_rows = lax.psum(margin_part, 'domain')]
    dot_general x1 -> x4, matrix products: 4.98 us -> 11.3 us  [per_device(): lax.dot_general(last, gathered[b], contract, preferred_element_type=jnp.f...]
  transfers between devices with their start and end apart: 4 -> 5, of which waited for: 3 -> 4; matrix products, arithmetic and copies ran while one was open for 0% -> 1% of each run, Pallas kernels for 35% -> 22%
where the time goes in v2:
time: 429 us; the launch traced here: 428 us
  waiting for transfers between devices  193 us (45%)
  Pallas kernels  160 us (37%)
  matrix products  37.7 us (9%)
  between operations  16.7 us (4%)
  local copies, waits for them, and re-layouts  15.2 us (4%)
  other arithmetic  5.85 us (1%)
    pallas_call x2, Pallas kernels, chain(): pl.pallas_call(functools.partial(chain_kernel, steps, plain, count, half_...  86 us
    psum x1, waiting for transfers between devices, per_device(): margin_rows = lax.psum(margin_part, 'domain')  78.1 us
    pallas_call x2, Pallas kernels, cholesky_inverse(): pl.pallas_call(functools.partial(inverse_kernel, first, last), out_shape=...  73.6 us
    all_gather x1, waiting for transfers between devices, per_device(): lax.all_gather(last.reshape(cells * ROWS, columns), 'band', axis=0)  67.3 us
    psum x1, waiting for transfers between devices, per_device(): cross_cols = lax.psum(cross_part, 'domain')  32.2 us
    all_gather x1, waiting for transfers between devices, per_device(): lax.all_gather(margin_rows / total_rows, 'band', axis=0, tiled=True)  15.2 us
    dot_general x4, matrix products, per_device(): lax.dot_general(last, gathered[b], contract, preferred_element_type=jnp.f...  11.3 us
    dot_general x1, matrix products, per_device(): jnp.einsum('ik,bkj->ibj', mine, cross, precision=highest, preferred_eleme...  9.29 us
  transfers between devices with their start and end apart: 5, of which 4 were waited for; matrix products, arithmetic and copies ran while one was open for 1% of the time, Pallas kernels for 22%

profile of v2, /device:TPU:0, one launch (start us, length us, event | category | flops | bytes accessed | tf_op | source)
XLA Modules:
  0.0 428.3 jit_solution(14582309472261447894)
XLA Ops:
  7.2 0.0 all-gather.5.cloned.1.call-start
  7.2 1.3 fusion.17
  11.1 0.8 copy.37.refs_0_
  12.0 1.9 reshape.46
  13.9 0.0 copy-start.9
  13.9 0.1 reshape.47
  14.0 2.0 copy.38.refs_3_
  16.1 0.0 copy-done.9
  16.1 0.1 copy.35
  16.2 0.1 copy.36
  16.3 0.0 copy-start.8
  16.3 0.0 copy-start.2
  16.4 0.2 pad.12.refs_2_
  16.6 0.6 copy-done.8
  17.2 0.1 pad_maximum_fusion.1.refs_1_
  17.3 67.2 %chain.1.refs_2_ = bf16[32,128,256]{2,1,0:T(8,128)(2,1)} custom-call(s32[32,6]{1,0:T(8,128)S(1)} %copy.37.refs_0_, f32[3]{0:T(128)S(1)} %pad_maximum_fusion.1.refs_1_, bf16[32,128,256]{2,1,0:T(8,128)(2,1)S(1)} %pad.12.refs_2_, f32[32,128,1]{2,1,0:T(8,128)} %copy.38.refs_3_, bf16[128,320]{1,0:T(8,128)(2,1)S(1)} %fusion.13.refs_4_, bf16[192,128]{1,0:T(8,128)(2,1)S(1)} %copy-done.2), custom_call_target="tpu_custom_call" | custom-call | flops 4294967296 | bytes 67108864 | tf_op jit(solution)/shard_map/chain/pallas_call | solution.py:138
  84.5 0.0 all-gather.5.cloned.1.call-update
  84.5 0.0 all-reduce.6.cloned.1.call-start
  84.6 67.3 %all-gather.5.cloned.1.call-done = bf16[4,4096,256]{2,1,0:T(8,128)(2,1)} async-done(((bf16[1,4096,256]{2,1,0:T(8,128)(2,1)}), bf16[4,4096,256]{2,1,0:T(8,128)(2,1)}) %all-gather.5.cloned.1.call-update) | async-done | bytes 8388624 | tf_op jit(solution)/shard_map/all_gather | solution.py:277
  151.9 3.1 fusion.1
  155.0 3.5 fusion.2
  158.5 2.3 fusion.3
  160.8 2.3 fusion.4
  163.2 1.1 pad_maximum_fusion
  164.3 0.0 all-reduce.6.cloned.1.call-update
  164.3 0.0 all-gather.7.cloned.1.call-start
  164.4 78.1 %all-reduce.6.cloned.1.call-done = f32[256,1024]{1,0:T(8,128)} async-done(((f32[256,1024]{1,0:T(8,128)}), f32[256,1024]{1,0:T(8,128)}) %all-reduce.6.cloned.1.call-update) | async-done | bytes 1048592 | tf_op jit(solution)/shard_map/psum | solution.py:292
  242.4 2.3 broadcast_multiply_fusion.1
  244.8 0.0 all-gather.7.cloned.1.call-update
  244.8 0.2 all-reduce.8.cloned.1.call-start
  245.0 18.8 %image.1 = bf16[32,128,256]{2,1,0:T(8,128)(2,1)S(1)} custom-call(s32[32,6]{1,0:T(8,128)S(1)} %copy.37.refs_0_, f32[3]{0:T(128)S(1)} %pad_maximum_fusion.1.refs_1_, bf16[32,128,256]{2,1,0:T(8,128)(2,1)} %chain.1.refs_2_, f32[32,128,1]{2,1,0:T(8,128)} %copy.38.refs_3_, bf16[128,320]{1,0:T(8,128)(2,1)S(1)} %fusion.13.refs_4_, bf16[192,128]{1,0:T(8,128)(2,1)S(1)} %copy-done.2), custom_call_target="tpu_custom_call" | custom-call | flops 1073741824 | bytes 16777216 | tf_op jit(solution)/shard_map/image/pallas_call | solution.py:138
  263.8 15.2 %all-gather.7.cloned.1.call-done.source_ref = f32[1024,1024]{1,0:T(8,128)} async-done(((f32[256,1024]{1,0:T(8,128)}), f32[1024,1024]{1,0:T(8,128)}) %all-gather.7.cloned.1.call-update) | async-done | bytes 4194320 | tf_op jit(solution)/shard_map/all_gather | solution.py:293
  279.0 6.7 %fusion.5 = f32[4,256,256]{2,1,0:T(8,128)} fusion(bf16[4,4096,256]{2,1,0:T(8,128)(2,1)} %all-gather.5.cloned.1.call-done, bf16[4096,256]{1,0:T(8,128)(2,1)S(1)} %bitcast.51), kind=kOutput, calls=%fused_computation.10 | convolution fusion | flops 2147483648 | bytes 11534336 | tf_op jit(solution)/shard_map/bni,nj->bij/dot_general | solution.py:295
  285.8 0.0 all-reduce.8.cloned.1.call-update
  285.8 0.0 all-gather.9.cloned.1.call-start
  285.9 2.2 copy-done.3
  288.0 41.9 %cholesky_inverse.2.source_ref = f32[1024,1024]{1,0:T(8,128)S(1)} custom-call(f32[1024,1024]{1,0:T(8,128)S(1)} %copy-done.3), custom_call_target="tpu_custom_call" | custom-call | flops 80530636800 | bytes 8388608 | tf_op jit(solution)/shard_map/cholesky_inverse/pallas_call | solution.py:241
  329.9 1.9 copy-done.4
  331.8 32.2 %all-reduce.8.cloned.1.call-done = f32[1024,256]{1,0:T(8,128)} async-done(((f32[1024,256]{1,0:T(8,128)}), f32[1024,256]{1,0:T(8,128)}) %all-reduce.8.cloned.1.call-update) | async-done | bytes 1048592 | tf_op jit(solution)/shard_map/psum | solution.py:298
  364.1 2.3 broadcast_multiply_fusion
  366.3 0.0 all-gather.9.cloned.1.call-update
  366.4 2.2 copy-done.5
  368.6 31.7 %cholesky_inverse.3 = f32[1024,1024]{1,0:T(8,128)S(1)} custom-call(f32[1024,1024]{1,0:T(8,128)S(1)} %copy-done.5), custom_call_target="tpu_custom_call" | custom-call | flops 80530636800 | bytes 8388608 | tf_op jit(solution)/shard_map/cholesky_inverse/pallas_call | solution.py:241
  400.3 0.1 dynamic-slice_convert_fusion
  400.4 2.4 fusion
  402.8 1.6 reshape.53
  404.4 9.3 %fusion.7 = f32[256,4,256]{0,2,1:T(8,128)S(1)} fusion(f32[4,1024,256]{2,1,0:T(8,128)} %bitcast.52, f32[1024,1024]{1,0:T(8,128)} %copy-done, s32[]{:T(128)S(6)} %select_n.3), kind=kOutput, calls=%fused_computation.13 | convolution fusion | flops 3221225472 | bytes 6291460 | tf_op jit(solution)/shard_map/ik,bkj->ibj/dot_general | solution.py:312
  413.7 8.0 %fusion.18 = f32[256,1024]{1,0:T(8,128)} fusion(f32[256,1024]{0,1:T(8,128)S(1)} %bitcast.53, f32[1024,1024]{1,0:T(8,128)S(1)} %copy-done.1), kind=kOutput, calls=%fused_computation.31 | convolution fusion | flops 3221225472 | bytes 6291456 | tf_op jit(solution)/shard_map/dot_general | solution.py:315
  (20 shorter events, 0.1 us)
Async XLA Ops:
  7.2 6.7 %copy-start.10 = (f32[4000]{0:T(1024)S(1)}, f32[4000]{0:T(1024)}, u32[]{:S(2)}) copy-start(f32[4000]{0:T(1024)} %param.9) | copy-start | bytes 48004
  7.2 144.7 %all-gather.5.cloned.1.call-start = ((), (), s32[]{:S(2)}) async-start(), calls=%async_computation | async-start | bytes 10485760 | tf_op jit(solution)/shard_map/all_gather | solution.py:277
  11.9 2.1 copy-start.11
  13.9 2.2 copy-start.9
  16.3 0.8 copy-start.8
  16.3 0.9 copy-start.2
  84.5 157.9 %all-reduce.6.cloned.1.call-start = ((), (), s32[]{:S(2)}) async-start(), calls=%async_computation.1 | async-start | bytes 2097152 | tf_op jit(solution)/shard_map/psum | solution.py:292
  151.9 6.6 %copy-start.6 = (bf16[4,4096,256]{2,1,0:T(8,128)(2,1)S(1)}, bf16[4,4096,256]{2,1,0:T(8,128)(2,1)}, u32[]{:S(2)}) copy-start(bf16[4,4096,256]{2,1,0:T(8,128)(2,1)} %all-gather.5.cloned.1.call-done) | copy-start | bytes 25165828
  164.3 114.7 %all-gather.7.cloned.1.call-start = ((), (), s32[]{:S(2)}) async-start(), calls=%async_computation.2 | async-start | bytes 5242880 | tf_op jit(solution)/shard_map/all_gather | solution.py:293
  244.8 119.2 %all-reduce.8.cloned.1.call-start = ((), (), s32[]{:S(2)}) async-start(), calls=%async_computation.3 | async-start | bytes 2097152 | tf_op jit(solution)/shard_map/psum | solution.py:298
  285.8 118.6 %all-gather.9.cloned.1.call-start = ((), (), s32[]{:S(2)}) async-start(), calls=%async_computation.4 | async-start | bytes 5242880 | tf_op jit(solution)/shard_map/all_gather | solution.py:302
  285.9 2.2 copy-start.3
  329.9 1.9 copy-start.4
  366.4 2.2 copy-start.5
  368.6 31.9 %copy-start.7 = (bf16[4,4096,256]{2,1,0:T(8,128)(2,1)S(1)}, bf16[4,4096,256]{2,1,0:T(8,128)(2,1)}, u32[]{:S(2)}) copy-start(bf16[4,4096,256]{2,1,0:T(8,128)(2,1)} %all-gather.5.cloned.1.call-done) | copy-start | bytes 25165828
  400.3 2.5 copy-start
  404.4 9.3 %copy-start.1 = (f32[1024,1024]{1,0:T(8,128)S(1)}, f32[1024,1024]{1,0:T(8,128)}, u32[]{:S(2)}) copy-start(f32[1024,1024]{1,0:T(8,128)} %copy-done) | copy-start | bytes 12582916
Sparse Core Ops, SparseCore 0:
  84.6 67.1 all-gather.4
  164.4 77.9 all-reduce.5
  244.9 34.0 all-gather.6
  285.9 78.0 all-reduce.7
  366.5 34.0 all-gather.8

commit v3 on v2

--- a/solution.py
+++ b/solution.py
@@ -246,7 +246,7 @@
         scratch_shapes=[pltpu.VMEM((BLOCK, size), jnp.float32)],
         compiler_params=pltpu.CompilerParams(vmem_limit_bytes=40 * 2**20),
         cost_estimate=pl.CostEstimate(
-            flops=75 * size**3, bytes_accessed=8 * size * size, transcendentals=size
+            flops=90 * size**3, bytes_accessed=8 * size * size, transcendentals=size
         ),
         name="cholesky_inverse",
     )(margin)
@@ -291,16 +291,13 @@
     )
     margin_rows = lax.psum(margin_part, "domain")
     margin = lax.all_gather(margin_rows / total_rows, "band", axis=0, tiled=True)
-    image, margin = lax.optimization_barrier((image, margin))
     cross_part = jnp.einsum(
         "bni,nj->bij", gathered, image, preferred_element_type=jnp.float32
     ).reshape(size, columns)
+    cross_part, margin = lax.optimization_barrier((cross_part, margin))
     cross_cols = lax.psum(cross_part, "domain")
-    blocks = size // BLOCK
-    begun = cholesky_inverse(margin, 0, blocks // 2)
-    cross_cols, begun = lax.optimization_barrier((cross_cols, begun))
-    cross = lax.all_gather(cross_cols / total_rows, "band", axis=0)
-    inverse = cholesky_inverse(begun, blocks // 2, blocks)
+    inverse = cholesky_inverse(margin, 0, size // BLOCK)
+    cross_cols, inverse = lax.optimization_barrier((cross_cols, inverse))
     mine = lax.dynamic_slice_in_dim(inverse, lax.axis_index("band") * columns, columns, 0)
     filtered = jnp.einsum(
         "bnj,kbj->nk",
@@ -309,9 +306,10 @@
         preferred_element_type=jnp.float32,
     ).astype(jnp.bfloat16)
     filtered = filtered.reshape(cells, ROWS, columns)[:, :NPC].reshape(nodes, columns)
-    left = jnp.einsum(
-        "ik,bkj->ibj", mine, cross, precision=highest, preferred_element_type=jnp.float32
-    ).reshape(columns, size)
+    left_cols = jnp.dot(
+        inverse, cross_cols / total_rows, precision=highest, preferred_element_type=jnp.float32
+    )
+    left = lax.all_to_all(left_cols, "band", split_axis=0, concat_axis=1, tiled=True)
     projected = lax.dot_general(
         left,
         inverse,

time: 429 us -> 404 us (0.942)
  waiting for transfers between devices: 193 us -> 153 us
  local copies, waits for them, and re-layouts: 15.2 us -> 27.5 us
    psum x1, waiting for transfers between devices: 32.2 us -> 1.71 us  [per_device(): cross_cols = lax.psum(cross_part, 'domain')]
    all_gather x1, waiting for transfers between devices: 15.2 us -> 0.01 us  [per_device(): lax.all_gather(margin_rows / total_rows, 'band', axis=0, tiled=True)]
    all_gather x0 -> x1, local copies, waits for them, and re-layouts: none -> 12 us  [per_device(): lax.all_gather(last.reshape(cells * ROWS, columns), 'band', axis=0)]
    all_to_all x0 -> x1, waiting for transfers between devices: none -> 5.51 us  [per_device(): lax.all_to_all(left_cols, 'band', split_axis=0, concat_axis=1, tiled=True)]
    pallas_call x2 -> x1, Pallas kernels: 73.6 us -> 73.3 us  [cholesky_inverse(): pl.pallas_call(functools.partial(inverse_kernel, first, last), out_shape=...]
  transfers between devices with their start and end apart: 5 -> 5, of which waited for: 4 -> 4; matrix products, arithmetic and copies ran while one was open for 1% -> 7% of each run, Pallas kernels for 22% -> 23%
where the time goes in v3:
time: 404 us; the launch traced here: 403 us
  Pallas kernels  159 us (39%)
  waiting for transfers between devices  153 us (38%)
  matrix products  39.3 us (10%)
  local copies, waits for them, and re-layouts  27.5 us (7%)
  between operations  16.7 us (4%)
  starting transfers between devices  4.08 us (1%)
    pallas_call x2, Pallas kernels, chain(): pl.pallas_call(functools.partial(chain_kernel, steps, plain, count, half_...  85.9 us
    psum x1, waiting for transfers between devices, per_device(): margin_rows = lax.psum(margin_part, 'domain')  78.2 us
    pallas_call x1, Pallas kernels, cholesky_inverse(): pl.pallas_call(functools.partial(inverse_kernel, first, last), out_shape=...  73.3 us
    all_gather x1, waiting for transfers between devices, per_device(): lax.all_gather(last.reshape(cells * ROWS, columns), 'band', axis=0)  67.3 us
    all_gather x1, local copies, waits for them, and re-layouts, per_device(): lax.all_gather(last.reshape(cells * ROWS, columns), 'band', axis=0)  12 us
    dot_general x4, matrix products, per_device(): lax.dot_general(last, gathered[b], contract, preferred_element_type=jnp.f...  11.3 us
    dot_general x1, matrix products, per_device(): lax.dot_general(left, inverse, (((1,), (1,)), ((), ())), precision=highes...  9.96 us
  transfers between devices with their start and end apart: 5, of which 4 were waited for; matrix products, arithmetic and copies ran while one was open for 7% of the time, Pallas kernels for 23%

profile of v3, /device:TPU:0, one launch (start us, length us, event | category | flops | bytes accessed | tf_op | source)
XLA Modules:
  0.0 403.2 jit_solution(10406800901540752039)
XLA Ops:
  7.2 0.0 copy-start.6
  7.2 0.0 all-gather.3.cloned.1.call-start
  7.2 1.3 fusion.15
  11.1 0.8 copy.34.refs_0_
  12.0 1.9 reshape.45
  13.9 0.0 copy-done.6
  13.9 0.0 copy-start.5
  13.9 0.1 reshape.46
  14.0 0.0 copy-done.7
  14.0 2.0 copy.35.refs_3_
  16.0 0.1 copy.32
  16.2 0.1 copy.33
  16.3 0.0 copy-start.4
  16.3 0.0 copy-start.1
  16.3 0.2 pad.12.refs_2_
  16.6 0.6 copy-done.4
  17.2 0.1 pad_maximum_fusion.1.refs_1_
  17.3 67.2 %chain.1.refs_2_ = bf16[32,128,256]{2,1,0:T(8,128)(2,1)} custom-call(s32[32,6]{1,0:T(8,128)S(1)} %copy.34.refs_0_, f32[3]{0:T(128)S(1)} %pad_maximum_fusion.1.refs_1_, bf16[32,128,256]{2,1,0:T(8,128)(2,1)S(1)} %pad.12.refs_2_, f32[32,128,1]{2,1,0:T(8,128)} %copy.35.refs_3_, bf16[128,320]{1,0:T(8,128)(2,1)S(1)} %fusion.11.refs_4_, bf16[192,128]{1,0:T(8,128)(2,1)S(1)} %copy-done.1), custom_call_target="tpu_custom_call" | custom-call | flops 4294967296 | bytes 67108864 | tf_op jit(solution)/shard_map/chain/pallas_call | solution.py:138
  84.5 0.0 all-gather.3.cloned.1.call-update
  84.5 0.0 all-reduce.6.cloned.1.call-start
  84.5 67.3 %all-gather.3.cloned.1.call-done = bf16[4,4096,256]{2,1,0:T(8,128)(2,1)} async-done(((bf16[1,4096,256]{2,1,0:T(8,128)(2,1)}), bf16[4,4096,256]{2,1,0:T(8,128)(2,1)}) %all-gather.3.cloned.1.call-update) | async-done | bytes 8388624 | tf_op jit(solution)/shard_map/all_gather | solution.py:277
  151.8 3.1 fusion.1
  155.0 3.5 fusion.2
  158.5 2.3 fusion.3
  160.8 2.3 fusion.4
  163.2 1.1 pad_maximum_fusion
  164.3 0.0 all-reduce.6.cloned.1.call-update
  164.3 0.0 all-gather.5.cloned.1.call-start
  164.3 78.2 %all-reduce.6.cloned.1.call-done = f32[256,1024]{1,0:T(8,128)} async-done(((f32[256,1024]{1,0:T(8,128)}), f32[256,1024]{1,0:T(8,128)}) %all-reduce.6.cloned.1.call-update) | async-done | bytes 1048592 | tf_op jit(solution)/shard_map/psum | solution.py:292
  242.6 2.3 broadcast_multiply_fusion
  244.9 0.0 all-gather.5.cloned.1.call-update
  244.9 0.2 all-reduce.8.cloned.1.call-start
  245.2 18.8 %image.1 = bf16[32,128,256]{2,1,0:T(8,128)(2,1)S(1)} custom-call(s32[32,6]{1,0:T(8,128)S(1)} %copy.34.refs_0_, f32[3]{0:T(128)S(1)} %pad_maximum_fusion.1.refs_1_, bf16[32,128,256]{2,1,0:T(8,128)(2,1)} %chain.1.refs_2_, f32[32,128,1]{2,1,0:T(8,128)} %copy.35.refs_3_, bf16[128,320]{1,0:T(8,128)(2,1)S(1)} %fusion.11.refs_4_, bf16[192,128]{1,0:T(8,128)(2,1)S(1)} %copy-done.1), custom_call_target="tpu_custom_call" | custom-call | flops 1073741824 | bytes 16777216 | tf_op jit(solution)/shard_map/image/pallas_call | solution.py:138
  263.9 12.0 %copy.36 = bf16[4,4096,256]{1,2,0:T(8,128)(2,1)} copy(bf16[4,4096,256]{2,1,0:T(8,128)(2,1)} %all-gather.3.cloned.1.call-done) | data formatting | bytes 16777216 | tf_op jit(solution)/shard_map/all_gather | solution.py:277
  275.9 6.7 %fusion.16 = f32[1024,256]{1,0:T(8,128)} fusion(bf16[1024,4096]{1,0:T(8,128)(2,1)} %bitcast.51, bf16[4096,256]{1,0:T(8,128)(2,1)S(1)} %bitcast.50), kind=kOutput, calls=%fused_computation.28 | convolution fusion | flops 2147483648 | bytes 11534336 | tf_op jit(solution)/shard_map/bni,nj->bij/dot_general | solution.py:294
  282.7 0.0 all-reduce.8.cloned.1.call-update
  282.7 2.2 copy-done.2
  284.9 73.3 %cholesky_inverse.1 = f32[1024,1024]{1,0:T(8,128)S(1)} custom-call(f32[1024,1024]{1,0:T(8,128)S(1)} %copy-done.2), custom_call_target="tpu_custom_call" | custom-call | flops 96636764160 | bytes 8388608 | tf_op jit(solution)/shard_map/cholesky_inverse/pallas_call | solution.py:241
  358.2 2.0 copy-done
  360.2 1.7 all-reduce.8.cloned.1.call-done
  361.9 5.5 %fusion.5 = f32[1024,256]{1,0:T(8,128)S(1)} fusion(f32[1024,1024]{1,0:T(8,128)} %copy-done, f32[1024,256]{1,0:T(8,128)} %all-reduce.8.cloned.1.call-done), kind=kOutput, calls=%fused_computation.11 | convolution fusion | flops 3221487616 | bytes 6291456 | tf_op jit(solution)/shard_map/dot_general | solution.py:309
  367.4 1.3 copy.44
  368.8 3.7 all-to-all-start
  372.5 1.3 dynamic-slice_convert_fusion
  373.8 5.8 %fusion = bf16[4096,256]{1,0:T(8,128)(2,1)S(1)} fusion(bf16[4,4096,256]{2,1,0:T(8,128)(2,1)} %all-gather.3.cloned.1.call-done, bf16[32,4,8,256]{3,2,1,0:T(8,128)(2,1)S(1)} %bitcast.55), kind=kOutput, calls=%fused_computation.1 | convolution fusion | flops 2148532224 | bytes 11010048 | tf_op jit(solution)/shard_map/bnj,kbj->nk/dot_general | solution.py:302
  379.6 1.6 reshape.51
  381.2 5.5 %all-to-all-done = f32[4,256,256]{1,2,0:T(8,128)S(1)} async-done(((f32[4,256,256]{1,2,0:T(8,128)}), f32[4,256,256]{1,2,0:T(8,128)S(1)}, u32[]{:S(2)}, u32[]{:S(2)}) %all-to-all-start) | async-done | bytes 1048608 | tf_op jit(solution)/shard_map/all_to_all | solution.py:312
  386.7 10.0 %fusion.17 = f32[256,1024]{1,0:T(8,128)} fusion(f32[256,1024]{0,1:T(8,128)S(1)} %bitcast.52, f32[1024,1024]{1,0:T(8,128)} %copy-done), kind=kOutput, calls=%fused_computation.29 | convolution fusion | flops 3221225472 | bytes 6291456 | tf_op jit(solution)/shard_map/dot_general | solution.py:313
  (11 shorter events, 0.1 us)
Async XLA Ops:
  7.2 6.7 %copy-start.6 = (f32[4000]{0:T(1024)S(1)}, f32[4000]{0:T(1024)}, u32[]{:S(2)}) copy-start(f32[4000]{0:T(1024)} %param.9) | copy-start | bytes 48004
  7.2 144.7 %all-gather.3.cloned.1.call-start = ((), (), s32[]{:S(2)}) async-start(), calls=%async_computation.1 | async-start | bytes 10485760 | tf_op jit(solution)/shard_map/all_gather | solution.py:277
  11.9 2.1 copy-start.7
  13.9 2.2 copy-start.5
  16.3 0.8 copy-start.4
  16.3 0.9 copy-start.1
  84.5 158.1 %all-reduce.6.cloned.1.call-start = ((), (), s32[]{:S(2)}) async-start(), calls=%async_computation.2 | async-start | bytes 2097152 | tf_op jit(solution)/shard_map/psum | solution.py:292
  151.8 6.6 %copy-start.3 = (bf16[4,4096,256]{2,1,0:T(8,128)(2,1)S(1)}, bf16[4,4096,256]{2,1,0:T(8,128)(2,1)}, u32[]{:S(2)}) copy-start(bf16[4,4096,256]{2,1,0:T(8,128)(2,1)} %all-gather.3.cloned.1.call-done) | copy-start | bytes 25165828
  164.3 118.4 %all-gather.5.cloned.1.call-start = ((), (), s32[]{:S(2)}) async-start(), calls=%async_computation.3 | async-start | bytes 5242880 | tf_op jit(solution)/shard_map/all_gather | solution.py:293
  244.9 117.0 %all-reduce.8.cloned.1.call-start = ((), (), s32[]{:S(2)}) async-start(), calls=%async_computation.4 | async-start | bytes 2097152 | tf_op jit(solution)/shard_map/psum | solution.py:298
  282.7 2.2 copy-start.2
  358.2 2.0 copy-start
  368.8 18.0 %all-to-all-start = ((f32[4,256,256]{1,2,0:T(8,128)}), f32[4,256,256]{1,2,0:T(8,128)S(1)}, u32[]{:S(2)}, u32[]{:S(2)}) async-start(f32[4,256,256]{1,2,0:T(8,128)} %copy.44), calls=%async_computation | async-start | bytes 2097152 | tf_op jit(solution)/shard_map/all_to_all | solution.py:312
Sparse Core Ops, SparseCore 0:
  84.6 67.1 all-gather.2
  164.4 78.1 all-reduce.5
  245.1 34.0 all-gather.4
  283.5 78.3 all-reduce.7
